TPU v7x, 32 devices: a whole 2x2x4 slice. The times are simulated.
32 devices in a mesh: row: 4 (over y, core), col: 8 (over z, x).
Axes of the slice: x: 2, y: 2, z: 4, core: 2. Of those that a mesh axis runs over, the one named last changes fastest.
Arguments:
- mock_maps: bfloat16 [512, 40960], P('col', 'row'), may hold values from -6 to 6
- window_blocks: int32 [4], replicated, may hold values from 0 to 31, as said below
- kept_tiles: int32 [32, 4], P(('row', 'col')), may hold values from 0 to 1, as said below
- taper_index: int32 [32, 4], P(('row', 'col')), may hold values from 0 to 3, as said below
- taper_table: float32 [4], replicated, may hold values from 0.25 to 2
Outputs:
- covariance: bfloat16 [40960, 5120], P(('row', 'col'))
Inputs may be any that keep to these rules, and one draw needn't show every extreme that they name: `window_blocks`: the entries are distinct feature blocks; the first and the last feature block are always among them. `kept_tiles`: A tile whose row block is its own window column block is always kept. `taper_index`: A tile whose row block is its own window column block takes entry 0.
All inputs are finite; a program needn't handle non-finite values.
Results may differ from a plain program's by a relative error of at most 0.001.
Values may be sent and summed in bfloat16 or wider, within the bound.
A program may use at most 128 MiB of HBM per device.

v0:
```python
import functools

import jax
import jax.numpy as jnp
from jax import lax
from jax.experimental import pallas as pl
from jax.experimental.pallas import tpu as pltpu
from jax.sharding import PartitionSpec as P

MESH = pl.DeviceIdType.MESH
WINDOW = 4
CORES = 2
ALONG_Z = 4


def gather_kernel(
    row_count, col_count, window_ref, maps_ref, own_ref, panels_ref,
    maps, for_twin, mine, from_twin, summed, from_y, piece,
    twin_send, twin_recv, ysum_send, ysum_recv,
    z_send, x_send, y_send, core_send, panel_recv,
    own_send, own_recv, local_sem,
):
    ny, nx, nz = row_count // CORES, col_count // ALONG_Z, ALONG_Z
    row, col = lax.axis_index("row"), lax.axis_index("col")
    y, core = row // CORES, row % CORES
    z, x = col // nx, col % nx
    twin = y * CORES + (1 - core)
    width = own_ref.shape[2]
    part = panels_ref.shape[3]

    load_maps = pltpu.make_async_copy(maps_ref, maps, local_sem.at[2])
    load_maps.start()

    def row_of(d):
        return lax.rem(y + d, ny) * CORES + core

    barrier = pltpu.get_barrier_semaphore()
    peers = [(row, lax.rem(col + d, col_count)) for d in range(1, col_count)]
    peers += [(twin, col)] + [(row_of(d), col) for d in range(1, ny)]
    for peer in peers:
        pl.semaphore_signal(barrier, inc=1, device_id=peer, device_id_type=MESH)

    last = row_count * col_count - 1
    is_middle, rank, seen = [], [], 0
    for t in range(WINDOW):
        block = window_ref[t]
        is_middle.append(jnp.minimum(block, 1) * jnp.minimum(last - block, 1))
        rank.append(seen)
        seen = seen + is_middle[t]

    def masked(slot, offset):
        block = jnp.int32(0)
        for t in range(WINDOW):
            chosen = is_middle[t] * (1 - jnp.minimum(jnp.abs(rank[t] + 1 - slot), 1))
            block = block + chosen * window_ref[t]
        block = block + last * (1 - jnp.minimum(jnp.abs(slot - (WINDOW - 1)), 1))
        found = jnp.zeros((maps.shape[0], part), jnp.float32)
        for j in range(col_count):
            here = 1 - jnp.minimum(jnp.abs(block - (row * col_count + j)), 1)
            columns = maps[:, pl.ds(pl.multiple_of(j * width + offset, 128), part)]
            found = found + columns.astype(jnp.float32) * here.astype(jnp.float32)
        return found.astype(jnp.bfloat16)

    pl.semaphore_wait(barrier, len(peers))

    started = []

    def send(src, dst, send_sem, recv_sem, device):
        copy = pltpu.make_async_remote_copy(
            src_ref=src, dst_ref=dst, send_sem=send_sem, recv_sem=recv_sem,
            device_id=device, device_id_type=MESH,
        )
        copy.start()
        return copy

    def send_own(d):
        dest = lax.rem(col + d, col_count)
        columns = pl.ds(pl.multiple_of(dest * width, 128), width)
        started.append(send(
            maps_ref.at[:, columns], own_ref.at[col],
            own_send.at[d], own_recv.at[col], (row, dest),
        ))

    pending = sorted(range(1, col_count), key=lambda d: (d % nx != 0, abs(d - col_count // 2)))
    along_z = sum(d % nx == 0 for d in pending)

    def send_some(count):
        for _ in range(min(count, len(pending))):
            send_own(pending.pop(0))

    def slot(r, c):
        return panels_ref.at[r, c]

    def arrived(r, c):
        pltpu.make_async_remote_copy(
            src_ref=slot(r, c), dst_ref=slot(r, c), send_sem=core_send.at[r, c],
            recv_sem=panel_recv.at[r, c], device_id=(row, col), device_id_type=MESH,
        ).wait_recv()

    def out(src, r, c, send_sem, device, waiting):
        copy = pltpu.make_async_remote_copy(
            src_ref=src, dst_ref=slot(r, c), send_sem=send_sem,
            recv_sem=panel_recv.at[r, c], device_id=device, device_id_type=MESH,
        )
        if waiting:
            copy.wait_send()
        else:
            copy.start()

    def z_out(src, zz, up, waiting):
        to = z + 1 if up else z - 1

        @pl.when(to < nz if up else to >= 0)
        def _():
            c = zz * nx + x
            out(src, row, c, z_send.at[int(up), zz], (row, to * nx + x), waiting)

    def x_out(src, zz, waiting):
        c = zz * nx + x
        for d in range(1, nx):
            out(src, row, c, x_send.at[d, zz], (row, z * nx + lax.rem(x + d, nx)), waiting)

    def y_out(src, c, waiting):
        for d in range(1, ny):
            out(src, row, c, y_send.at[d, c], (row_of(d), col), waiting)

    def core_out(src, r, c, waiting):
        out(src, r, c, core_send.at[r, c], (twin, col), waiting)

    def at_z(d, body):
        if d == 0:
            body(z, None)
            return

        @pl.when(z >= d)
        def _():
            body(z - d, True)

        @pl.when(z + d < nz)
        def _():
            body(z + d, False)

    def own_event(src, waiting):
        z_out(src, z, True, waiting)
        z_out(src, z, False, waiting)
        y_out(src, col, waiting)
        x_out(src, z, waiting)
        core_out(src, row, col, waiting)

    def z_event(waiting, zz, up):
        c = zz * nx + x
        src = slot(row, c)
        if not waiting:
            arrived(row, c)
        z_out(src, zz, up, waiting)
        y_out(src, c, waiting)
        x_out(src, zz, waiting)
        core_out(src, row, c, waiting)

    def x_event(waiting, zz, up):
        for d in range(1, nx):
            c = zz * nx + lax.rem(x + d, nx)
            if not waiting:
                arrived(row, c)
            y_out(slot(row, c), c, waiting)
            core_out(slot(row, c), row, c, waiting)

    def y_event(waiting, own_x, zz, up):
        for dx in ([0] if own_x else range(1, nx)):
            c = zz * nx + lax.rem(x + dx, nx)
            for d in range(1, ny):
                r = row_of(d)
                if not waiting:
                    arrived(r, c)
                core_out(slot(r, c), r, c, waiting)

    def events(waiting):
        if waiting:
            own_event(piece, True)
        for d in range(1, nz):
            at_z(d, functools.partial(z_event, waiting))
            if d == nz - 2 and not waiting:
                send_some(along_z)
            at_z(d - 1, functools.partial(x_event, waiting))
        if not waiting:
            send_some(col_count)
        at_z(nz - 1, functools.partial(x_event, waiting))
        for d in range(nz):
            at_z(d, functools.partial(y_event, waiting, True))
            at_z(d, functools.partial(y_event, waiting, False))

    keep_own = pltpu.make_async_copy(
        maps_ref.at[:, pl.ds(pl.multiple_of(col * width, 128), width)], own_ref.at[col], local_sem.at[0]
    )
    keep_own.start()
    direct = part == width and row_count == WINDOW
    ends = lax.rem(row, row_count - 1) == 0

    def y_sum(d):
        return pltpu.make_async_remote_copy(
            src_ref=summed.at[d], dst_ref=from_y.at[ny - d], send_sem=ysum_send.at[d],
            recv_sem=ysum_recv.at[ny - d], device_id=(row_of(d), col), device_id_type=MESH,
        )

    if direct:
        first = pl.multiple_of((row // (row_count - 1)) * ((col_count - 1) * width), 128)
        held_piece = maps_ref.at[:, pl.ds(first, width)]

        @pl.when(ends)
        def _():
            own_event(held_piece, False)
            pltpu.make_async_copy(held_piece, slot(row, col), local_sem.at[1]).start()

        load_maps.wait()
        for_twin[0] = masked(1 + core, 0)
        mine[0] = masked(2 - core, 0)
        twin_copy = send(for_twin, from_twin, twin_send, twin_recv, (twin, col))
        twin_copy.wait_recv()
        summed[1] = mine[0] + from_twin[0]

        @pl.when(ends)
        def _():
            y_sum(1).start()

        @pl.when(jnp.logical_not(ends))
        def _():
            y_sum(1).wait_recv()
            piece[...] = summed[1] + from_y[1]
            own_event(piece, False)
            pltpu.make_async_copy(piece, slot(row, col), local_sem.at[1]).start()
    else:
        load_maps.wait()
        for d in range(ny):
            for k, held in ((1 - core, for_twin), (core, mine)):
                first = (lax.rem(y + d, ny) * CORES + k) * part
                held[d] = masked(first // width, lax.rem(first, width))
        twin_copy = send(for_twin, from_twin, twin_send, twin_recv, (twin, col))
        twin_copy.wait_recv()
        for d in range(ny):
            summed[d] = mine[d] + from_twin[d]
        for d in range(1, ny):
            y_sum(d).start()
        total = summed[0]
        for d in range(1, ny):
            y_sum(d).wait_recv()
            total = total + from_y[ny - d]
        piece[...] = total
        own_event(piece, False)
        pltpu.make_async_copy(piece, slot(row, col), local_sem.at[1]).start()
    events(False)

    for d in range(ny):
        r = lax.rem(y + d, ny) * CORES + (1 - core)

        @pl.loop(0, col_count)
        def _(c):
            arrived(r, c)

    for d in range(1, col_count):
        source = lax.rem(col + d, col_count)
        pltpu.make_async_remote_copy(
            src_ref=own_ref.at[source], dst_ref=own_ref.at[source], send_sem=own_send.at[d],
            recv_sem=own_recv.at[source], device_id=(row, source), device_id_type=MESH,
        ).wait_recv()
    twin_copy.wait_send()
    for copy in started:
        copy.wait_send()
    if direct:
        @pl.when(ends)
        def _():
            y_sum(1).wait_send()
    else:
        for d in range(1, ny):
            y_sum(d).wait_send()
    events(True)
    keep_own.wait()
    pltpu.make_async_copy(piece, slot(row, col), local_sem.at[1]).wait()


def gather(mock_maps, window_blocks, row_count, col_count):
    mocks = mock_maps.shape[0]
    width = mock_maps.shape[1] // col_count
    part = WINDOW * width // row_count
    ny = row_count // CORES
    nx = col_count // ALONG_Z
    dma = pltpu.SemaphoreType.DMA
    shares = 1 if part == width else ny
    return pl.pallas_call(
        functools.partial(gather_kernel, row_count, col_count),
        out_shape=(
            jax.ShapeDtypeStruct((col_count, mocks, width), jnp.bfloat16),
            jax.ShapeDtypeStruct((row_count, col_count, mocks, part), jnp.bfloat16),
        ),
        in_specs=[pl.BlockSpec(memory_space=pltpu.SMEM), pl.BlockSpec(memory_space=pl.ANY)],
        out_specs=(pl.BlockSpec(memory_space=pl.ANY), pl.BlockSpec(memory_space=pl.ANY)),
        scratch_shapes=[
            pltpu.VMEM(mock_maps.shape, jnp.bfloat16),
            pltpu.VMEM((shares, mocks, part), jnp.bfloat16),
            pltpu.VMEM((shares, mocks, part), jnp.bfloat16),
            pltpu.VMEM((shares, mocks, part), jnp.bfloat16),
            pltpu.VMEM((ny, mocks, part), jnp.bfloat16),
            pltpu.VMEM((ny, mocks, part), jnp.bfloat16),
            pltpu.VMEM((mocks, part), jnp.bfloat16),
            dma, dma, dma((ny,)), dma((ny,)),
            dma((2, ALONG_Z)), dma((nx, ALONG_Z)), dma((ny, col_count)),
            dma((row_count, col_count)), dma((row_count, col_count)),
            dma((col_count,)), dma((col_count,)), dma((3,)),
        ],
        compiler_params=pltpu.CompilerParams(
            collective_id=0, has_side_effects=True, vmem_limit_bytes=60 * 2**20
        ),
        name="gather",
    )(window_blocks, mock_maps)


def ordered_slot(window_ref, last, slot):
    block = window_ref[slot]
    rank = jnp.int32(1)
    for t in range(WINDOW):
        middle = (t < slot) & (window_ref[t] != 0) & (window_ref[t] != last)
        rank = rank + middle.astype(jnp.int32)
    return jnp.where(block == 0, 0, jnp.where(block == last, WINDOW - 1, rank))


ONES = 16
HALVES = 2


def tile_kernel(
    parts, last, window_hbm, kept_hbm, index_hbm, table_hbm, own_hbm, panels_hbm, out_ref,
    window_ref, kept_ref, index_ref, table_ref, own_ref, panels_ref, own_t, own_sum, small_sem, own_sem, panel_sem,
):
    step, half = pl.program_id(0), pl.program_id(1)
    slot = step // parts
    count, width = own_ref.shape
    rows = width // HALVES
    steps = panels_ref.shape[0]

    def fetch(i):
        entry = ordered_slot(window_ref, last, i // parts) * parts + i % parts
        return pltpu.make_async_copy(panels_hbm.at[entry], panels_ref.at[i], panel_sem.at[i])

    @pl.when((step == 0) & (half == 0))
    def _():
        small = ((window_hbm, window_ref), (kept_hbm, kept_ref), (index_hbm, index_ref), (table_hbm, table_ref))
        copies = [pltpu.make_async_copy(src, dst, small_sem.at[i]) for i, (src, dst) in enumerate(small)]
        load_own = pltpu.make_async_copy(own_hbm, own_ref, own_sem)
        for copy in copies:
            copy.start()
        load_own.start()
        for copy in copies:
            copy.wait()
        for i in range(steps):
            @pl.when(kept_ref[0, i // parts] > 0)
            def _():
                fetch(i).start()
        load_own.wait()
        for h in range(HALVES):
            own_t[h, :ONES] = jnp.ones((ONES, count), jnp.bfloat16)
            own_t[h, ONES:] = own_ref[:, h * rows:(h + 1) * rows].T
            own_sum[h] = jnp.dot(
                own_t[h, ONES:], jnp.ones((count, 128), jnp.bfloat16), preferred_element_type=jnp.float32
            )

    kept = kept_ref[0, slot] > 0

    @pl.when(kept & (half == 0))
    def _():
        fetch(step).wait()

    @pl.when(kept)
    def _():
        scale = table_ref[index_ref[0, slot]] / (count - 1)
        panel = panels_ref[step]
        panel_mean = None
        for first in range(0, rows, rows // 2):
            skip = ONES if panel_mean is None else 0
            left = own_t[half, pl.ds(first + ONES - skip, rows // 2 + skip)]
            products = jnp.dot(left, panel, preferred_element_type=jnp.float32)
            if panel_mean is None:
                panel_mean = products[:1] * (scale / count)
            sums = own_sum[half, pl.ds(first, rows // 2)]
            for part in range(0, panel.shape[1], 128):
                here = slice(part, part + 128)
                value = scale * products[skip:, here] - sums * panel_mean[:, here]
                out_ref[first:first + rows // 2, here] = value.astype(jnp.bfloat16)

    @pl.when(jnp.logical_not(kept))
    def _():
        out_ref[...] = jnp.zeros_like(out_ref)


def tiles(own, panels, window_blocks, kept_tiles, taper_index, taper_table, last):
    count, width = own.shape
    steps, _, part = panels.shape
    parts = width // part
    dma = pltpu.SemaphoreType.DMA
    return pl.pallas_call(
        functools.partial(tile_kernel, parts, last),
        out_shape=jax.ShapeDtypeStruct((width, steps * part), jnp.bfloat16),
        grid=(steps, HALVES),
        in_specs=[pl.BlockSpec(memory_space=pl.ANY)] * 6,
        out_specs=pl.BlockSpec((width // HALVES, part), lambda i, h: (h, i)),
        scratch_shapes=[
            pltpu.SMEM(window_blocks.shape, jnp.int32),
            pltpu.SMEM(kept_tiles.shape, jnp.int32),
            pltpu.SMEM(taper_index.shape, jnp.int32),
            pltpu.SMEM(taper_table.shape, jnp.float32),
            pltpu.VMEM(own.shape, jnp.bfloat16),
            pltpu.VMEM(panels.shape, jnp.bfloat16),
            pltpu.VMEM((HALVES, ONES + width // HALVES, count), jnp.bfloat16),
            pltpu.VMEM((HALVES, width // HALVES, 128), jnp.float32),
            dma((4,)), dma, dma((steps,)),
        ],
        compiler_params=pltpu.CompilerParams(
            dimension_semantics=("arbitrary", "arbitrary"), vmem_limit_bytes=60 * 2**20
        ),
        name="tiles",
    )(window_blocks, kept_tiles, taper_index, taper_table, own, panels)


def per_device(row_count, col_count, mock_maps, window_blocks, kept_tiles, taper_index, taper_table):
    own, panels = gather(mock_maps, window_blocks, row_count, col_count)
    own = own.reshape(-1, own.shape[-1])
    panels = panels.reshape(panels.shape[0], -1, panels.shape[-1])
    last = row_count * col_count - 1
    return tiles(own, panels, window_blocks, kept_tiles, taper_index, taper_table, last)


def solution(mesh):
    in_specs = (P("col", "row"), P(), P(("row", "col"), None), P(("row", "col"), None), P())
    out_specs = P(("row", "col"), None)
    return jax.shard_map(
        functools.partial(per_device, mesh.shape["row"], mesh.shape["col"]),
        mesh=mesh, in_specs=in_specs, out_specs=out_specs, check_vma=False,
    )
```

profile of v0, /device:TPU:27, one launch (start us, length us, event | category | flops | bytes accessed | tf_op | source)
XLA Modules:
  0.0 63.6 jit_solution(17095733536364438868)
XLA Ops:
  0.0 52.2 %gather.1 = (bf16[8,64,1280]{2,1,0:T(8,128)(2,1)}, bf16[4,8,64,1280]{3,2,1,0:T(8,128)(2,1)}) custom-call(s32[4]{0:T(128)} %window_hbm.1, bf16[64,10240]{1,0:T(8,128)(2,1)} %maps_ref.1), custom_call_target="tpu_custom_call" | custom-call | tf_op jit(solution)/shard_map/gather/pallas_call | solution.py:288
  52.2 11.4 %tiles.1 = bf16[1280,5120]{1,0:T(8,128)(2,1)} custom-call(s32[4]{0:T(128)} %window_hbm.1, s32[1,4]{1,0:T(1,128)} %kept_hbm.1, s32[1,4]{1,0:T(1,128)} %index_hbm.1, f32[4]{0:T(128)} %table_hbm.1, bf16[512,1280]{1,0:T(8,128)(2,1)} %bitcast.3, bf16[4,512,1280]{2,1,0:T(8,128)(2,1)} %bitcast.2), custom_call_target="tpu_custom_call" | custom-call | tf_op jit(solution)/shard_map/tiles/pallas_call | solution.py:398
where the time goes:
time: 63.6 us
  Pallas kernels  63.6 us (100%)
    pallas_call x1, Pallas kernels, gather(): pl.pallas_call(functools.partial(gather_kernel, row_count, col_count), ou...  52.2 us
    pallas_call x1, Pallas kernels, tiles(): pl.pallas_call(functools.partial(tile_kernel, parts, last), out_shape=jax...  11.4 us

commit v1 on v0

--- a/solution.py
+++ b/solution.py
@@ -81,7 +81,10 @@
             own_send.at[d], own_recv.at[col], (row, dest),
         ))
 
-    pending = sorted(range(1, col_count), key=lambda d: (d % nx != 0, abs(d - col_count // 2)))
+    pending = sorted(
+        range(1, col_count),
+        key=lambda d: (1, abs(d - col_count // 2)) if d % nx else (0, -abs(d - col_count // 2)),
+    )
     along_z = sum(d % nx == 0 for d in pending)
 
     def send_some(count):
@@ -180,7 +183,7 @@
         for d in range(1, nz):
             at_z(d, functools.partial(z_event, waiting))
             if d == nz - 2 and not waiting:
-                send_some(along_z)
+                send_some(along_z - (2 if direct else 1))
             at_z(d - 1, functools.partial(x_event, waiting))
         if not waiting:
             send_some(col_count)
@@ -211,6 +214,7 @@
             own_event(held_piece, False)
             pltpu.make_async_copy(held_piece, slot(row, col), local_sem.at[1]).start()
 
+        send_some(1)
         load_maps.wait()
         for_twin[0] = masked(1 + core, 0)
         mine[0] = masked(2 - core, 0)
@@ -247,6 +251,7 @@
         piece[...] = total
         own_event(piece, False)
         pltpu.make_async_copy(piece, slot(row, col), local_sem.at[1]).start()
+    send_some(1)
     events(False)
 
     for d in range(ny):

time: 63.6 us -> 63.9 us (level)
  the two profiles are of different devices: /device:TPU:27 before, /device:TPU:1 now
where the time goes in v1:
time: 63.9 us; the launch traced here: 63.1 us
  Pallas kernels  63.1 us (99%)
    pallas_call x1, Pallas kernels, gather(): pl.pallas_call(functools.partial(gather_kernel, row_count, col_count), ou...  52 us
    pallas_call x1, Pallas kernels, tiles(): pl.pallas_call(functools.partial(tile_kernel, parts, last), out_shape=jax...  11 us

profile of v1, /device:TPU:1, one launch (start us, length us, event | category | flops | bytes accessed | tf_op | source)
XLA Modules:
  0.0 63.1 jit_solution(4853270480212536504)
XLA Ops:
  0.0 52.0 %gather.1 = (bf16[8,64,1280]{2,1,0:T(8,128)(2,1)}, bf16[4,8,64,1280]{3,2,1,0:T(8,128)(2,1)}) custom-call(s32[4]{0:T(128)} %window_hbm.1, bf16[64,10240]{1,0:T(8,128)(2,1)} %maps_ref.1), custom_call_target="tpu_custom_call" | custom-call | tf_op jit(solution)/shard_map/gather/pallas_call | solution.py:293
  52.0 11.0 %tiles.1 = bf16[1280,5120]{1,0:T(8,128)(2,1)} custom-call(s32[4]{0:T(128)} %window_hbm.1, s32[1,4]{1,0:T(1,128)} %kept_hbm.1, s32[1,4]{1,0:T(1,128)} %index_hbm.1, f32[4]{0:T(128)} %table_hbm.1, bf16[512,1280]{1,0:T(8,128)(2,1)} %bitcast.3, bf16[4,512,1280]{2,1,0:T(8,128)(2,1)} %bitcast.2), custom_call_target="tpu_custom_call" | custom-call | tf_op jit(solution)/shard_map/tiles/pallas_call | solution.py:403
